TPU v7x, 512 devices: a whole 4x8x8 slice. The times are simulated.
512 devices in a mesh: dp: 32 (over z, x), tensor: 16 (over y, core).
Axes of the slice: x: 4, y: 8, z: 8, core: 2. Of those that a mesh axis runs over, the one named last changes fastest.
Arguments:
- queries: bfloat16 [512, 256, 4096], P('dp', None, 'tensor'), may hold values from -250 to 250
- keys_values: bfloat16 [512, 256, 2, 512], P('dp', 'tensor'), may hold values from -50 to 50
- donors: int32 [512, 16], replicated, may hold values from 0 to 511, as said below
- ablated: int32 [16], replicated, may hold values from 0 to 31, as said below
Outputs:
- patched: bfloat16 [512, 256, 4096], P('dp', None, 'tensor')
Inputs may be any that keep to these rules, and one draw needn't show every extreme that they name: `ablated`: entry k lies among heads 2 * k to 2 * k + 1. For each column and each aligned block of 16 prompts, at most 1 of its donors lie in any one aligned block of 16 prompts, and exactly 1 in some.
All inputs are finite; a program needn't handle non-finite values.
Results may differ from a plain program's by a relative error of at most 0.0046.
Values may be sent and summed in bfloat16 or wider, within the bound.
A program may use at most 64 MiB of HBM per device.

v0:
```python
import math

import jax
import jax.numpy as jnp
from jax import lax
from jax.sharding import PartitionSpec as P

HSIZE = 128
GROUP = 8


def attend(query_rows, key_rows, value_rows):
    length = query_rows.shape[0]
    scores = jnp.einsum("shd,td->hst", query_rows, key_rows, preferred_element_type=jnp.float32) * (
        1.0 / math.sqrt(HSIZE)
    )
    causal = lax.broadcasted_iota(jnp.int32, (length, length), 0) >= lax.broadcasted_iota(
        jnp.int32, (length, length), 1
    )
    scores = jnp.where(causal[None], scores, -jnp.inf)
    row_max = jnp.max(scores, axis=2, keepdims=True)
    powers = jnp.exp(scores - row_max)
    weights = (powers / jnp.sum(powers, axis=2, keepdims=True)).astype(jnp.bfloat16)
    return jnp.einsum(
        "hst,td->shd", weights, value_rows, preferred_element_type=jnp.float32
    ).astype(jnp.bfloat16)


def attend_prompt(inputs):
    return attend(inputs[0], inputs[1], inputs[2])


def on_device(queries, keys_values, donors, ablated):
    tp_index = lax.axis_index("tensor")
    dp_index = lax.axis_index("dp")
    dp_count = lax.axis_size("dp")
    prompts_dev, length, row_width = queries.shape
    head_dev = row_width // HSIZE
    slot_count = max(1, prompts_dev // dp_count)
    gathered = lax.all_gather(keys_values, "tensor", axis=1, tiled=True)
    own_rows = lax.dynamic_slice_in_dim(gathered, tp_index * head_dev // GROUP * HSIZE, HSIZE, 3)
    key_rows = own_rows[:, :, 0]
    value_rows = own_rows[:, :, 1]
    per_head = queries.reshape(prompts_dev, length, head_dev, HSIZE)
    local_head = ablated[tp_index] - tp_index * head_dev
    column = lax.dynamic_index_in_dim(donors, tp_index, 1, keepdims=False)
    outputs = lax.map(attend_prompt, (per_head, key_rows, value_rows))
    head_block = lax.dynamic_index_in_dim(outputs, local_head, 2, keepdims=False)
    by_dest = column.reshape(dp_count, prompts_dev)
    source_dev = by_dest // prompts_dev
    source_row = by_dest % prompts_dev
    order_index = jnp.arange(prompts_dev)
    same_source = source_dev[:, :, None] == source_dev[:, None, :]
    before = (order_index[:, None] < order_index[None, :])[None]
    slot_rank = jnp.sum((same_source & before).astype(jnp.int32), axis=1)
    chosen = source_dev == dp_index
    slot_match = slot_rank[:, :, None] == jnp.arange(slot_count)[None, None, :]
    row_match = source_row[:, :, None] == order_index[None, None, :]
    matches = chosen[:, :, None, None] & slot_match[:, :, :, None] & row_match[:, :, None, :]
    selector = jnp.sum(matches.astype(jnp.float32), axis=1).astype(jnp.bfloat16)
    selector = selector.reshape(dp_count * slot_count, prompts_dev)
    outgoing = jnp.dot(
        selector,
        head_block.reshape(prompts_dev, length * HSIZE),
        preferred_element_type=jnp.float32,
    )
    outgoing = outgoing.astype(jnp.bfloat16).reshape(dp_count, slot_count, length, HSIZE)
    received = lax.all_to_all(outgoing, "dp", split_axis=0, concat_axis=0, tiled=True)
    own_source = lax.dynamic_index_in_dim(source_dev, dp_index, 0, keepdims=False)
    own_rank = lax.dynamic_index_in_dim(slot_rank, dp_index, 0, keepdims=False)
    slot_label = own_source * slot_count + own_rank
    picker = (slot_label[:, None] == jnp.arange(dp_count * slot_count)[None, :]).astype(
        jnp.bfloat16
    )
    replaced = jnp.dot(
        picker,
        received.reshape(dp_count * slot_count, length * HSIZE),
        preferred_element_type=jnp.float32,
    )
    outputs = lax.dynamic_update_index_in_dim(
        outputs, replaced.astype(jnp.bfloat16).reshape(prompts_dev, length, HSIZE), local_head, 2
    )
    return outputs.reshape(prompts_dev, length, head_dev * HSIZE)


def solution(mesh):
    return jax.shard_map(
        on_device,
        mesh=mesh,
        in_specs=(P("dp", None, "tensor"), P("dp", "tensor", None, None), P(), P()),
        out_specs=P("dp", None, "tensor"),
        check_vma=False,
    )
```

profile of v0, /device:TPU:5, one launch (start us, length us, event | category | flops | bytes accessed | tf_op | source)
XLA Modules:
  0.0 212.7 jit_solution(18169594065742528036)
XLA Ops:
  6.5 2.0 copy.40
  8.6 1.2 dynamic_slice.36
  10.5 3.9 %copy.41 = bf16[16,256,256]{1,2,0:T(8,128)(2,1)} copy(bf16[16,256,256]{2,1,0:T(8,128)(2,1)} %param.6) | data formatting | bytes 4194304 | tf_op args[0]
  14.8 58.0 %all-gather.2.cloned.1.call-done = bf16[16,256,2,512]{3,1,0,2:T(8,128)(2,1)} async-done(((bf16[16,16,2,512]{3,1,0,2:T(8,128)(2,1)}), bf16[16,256,2,512]{3,1,0,2:T(8,128)(2,1)}) %all-gather.2.cloned.1.call-update) | async-done | bytes 8388624 | tf_op jit(solution)/shard_map/all_gather | solution.py:40
  72.8 3.2 %dynamic-slice_bitcast_fusion = (bf16[16,256,128]{2,1,0:T(8,128)(2,1)}, bf16[16,256,128]{2,1,0:T(8,128)(2,1)}) fusion(bf16[16,256,2,512]{3,1,0,2:T(8,128)(2,1)} %all-gather.2.cloned.1.call-done, s32[]{:T(128)S(6)} %select_n.56, s32[]{:T(128)S(6)} %add.66), kind=kLoop, calls=%fused_computation.32 | loop fusion | bytes 4194312 | tf_op jit(solution)/shard_map/squeeze | solution.py:42
  76.0 57.9 %while.10 = (s32[]{:T(128)}, bf16[16,256,2,128]{1,3,2,0:T(8,128)(2,1)S(1)}, bf16[16,256,128]{2,1,0:T(8,128)(2,1)}, bf16[16,256,128]{2,1,0:T(8,128)(2,1)}, bf16[16,256,2,128]{1,3,2,0:T(8,128)(2,1)}, /*index=5*/s32[]{:T(128)}) while((s32[]{:T(128)}, bf16[16,256,2,128]{1,3,2,0:T(8,128)(2,1)S(1)}, bf16[16,256,128]{2,1,0:T(8,128)(2,1)}, ...), condition=%wide.region_3.4_spmd, body=%wide.region_0.3_spmd.sunk | while | flops 101975040 | bytes 2366533 | solution.py:47
  76.0 1.2 fusion.61
  77.2 1.3 fusion.60
  78.4 1.1 fusion.62
  79.6 1.2 fusion.61
  80.8 1.3 fusion.60
  82.1 1.1 fusion.62
  83.2 1.2 fusion.61
  84.4 1.3 fusion.60
  85.7 1.1 fusion.62
  86.8 1.2 fusion.61
  88.0 1.3 fusion.60
  89.3 1.1 fusion.62
  90.5 1.2 fusion.61
  91.6 1.3 fusion.60
  92.9 1.1 fusion.62
  94.1 1.2 fusion.61
  95.3 1.3 fusion.60
  96.5 1.1 fusion.62
  97.7 1.2 fusion.61
  98.9 1.3 fusion.60
  100.1 1.1 fusion.62
  101.3 1.2 fusion.61
  102.5 1.3 fusion.60
  103.8 1.1 fusion.62
  104.9 1.2 fusion.61
  106.1 1.3 fusion.60
  107.4 1.1 fusion.62
  108.6 1.2 fusion.61
  109.7 1.3 fusion.60
  111.0 1.1 fusion.62
  112.2 1.2 fusion.61
  113.3 1.3 fusion.60
  114.6 1.1 fusion.62
  115.8 1.2 fusion.61
  117.0 1.3 fusion.60
  118.2 1.1 fusion.62
  119.4 1.2 fusion.61
  120.6 1.3 fusion.60
  121.8 1.1 fusion.62
  123.0 1.2 fusion.61
  124.2 1.3 fusion.60
  125.5 1.1 fusion.62
  126.7 1.2 fusion.61
  127.8 1.3 fusion.60
  129.1 1.1 fusion.62
  130.3 1.2 fusion.61
  131.4 1.3 fusion.60
  132.7 1.1 fusion.62
  133.9 1.6 copy.48
  135.5 2.0 fusion.27
  137.6 1.8 copy.57
  139.4 9.9 %all-to-all-start = ((bf16[32,1,256,128]{3,2,1,0:T(8,128)(2,1)}), bf16[32,1,256,128]{3,2,1,0:T(8,128)(2,1)S(1)}, u32[]{:S(2)}, u32[]{:S(2)}) async-start(bf16[32,1,256,128]{3,2,1,0:T(8,128)(2,1)} %bitcast.88), calls=%async_computation | async-start | bytes 4194304 | tf_op jit(solution)/shard_map/all_to_all | solution.py:68
  149.3 0.2 add_reduce_fusion
  149.5 49.9 %all-to-all-done = bf16[32,1,256,128]{3,2,1,0:T(8,128)(2,1)S(1)} async-done(((bf16[32,1,256,128]{3,2,1,0:T(8,128)(2,1)}), bf16[32,1,256,128]{3,2,1,0:T(8,128)(2,1)S(1)}, u32[]{:S(2)}, u32[]{:S(2)}) %all-to-all-start) | async-done | bytes 2097184 | tf_op jit(solution)/shard_map/all_to_all | solution.py:68
  199.4 1.3 fusion.28
  200.7 1.2 copy.59
  201.9 1.5 copy.50
  203.5 2.4 %copy.53 = bf16[16,256,256]{2,1,0:T(8,128)(2,1)} copy(bf16[16,256,256]{1,2,0:T(8,128)(2,1)S(1)} %bitcast.89) | data formatting | bytes 4194304 | tf_op jit(solution)/shard_map/reshape | solution.py:83
  (35 shorter events, 1.0 us)
Async XLA Ops:
  6.5 7.9 %copy-start = (s32[512,16]{0,1:T(8,128)S(1)}, s32[512,16]{0,1:T(8,128)}, u32[]{:S(2)}) copy-start(s32[512,16]{0,1:T(8,128)} %param.8) | copy-start | bytes 98308
  6.5 66.3 %all-gather.2.cloned.1.call-start = ((), (), s32[]{:S(2)}) async-start(), calls=%async_computation.1 | async-start | bytes 8912896 | tf_op jit(solution)/shard_map/all_gather | solution.py:40
  133.8 1.7 copy-start.1
  139.4 60.0 %all-to-all-start = ((bf16[32,1,256,128]{3,2,1,0:T(8,128)(2,1)}), bf16[32,1,256,128]{3,2,1,0:T(8,128)(2,1)S(1)}, u32[]{:S(2)}, u32[]{:S(2)}) async-start(bf16[32,1,256,128]{3,2,1,0:T(8,128)(2,1)} %bitcast.88), calls=%async_computation | async-start | bytes 4194304 | tf_op jit(solution)/shard_map/all_to_all | solution.py:68
  200.7 2.7 %copy-start.2 = (bf16[16,256,2,128]{1,3,2,0:T(8,128)(2,1)S(1)}, bf16[16,256,2,128]{1,3,2,0:T(8,128)(2,1)}, u32[]{:S(2)}) copy-start(bf16[16,256,2,128]{1,3,2,0:T(8,128)(2,1)} %copy-done.1) | copy-start | bytes 6291460
Sparse Core Ops, SparseCore 0:
  9.5 63.2 all-gather.1
where the time goes:
time: 214 us; the launch traced here: 213 us
  waiting for transfers between devices  108 us (50%)
  matrix products  60.1 us (28%)
  local copies, waits for them, and re-layouts  19.1 us (9%)
  between operations  14.2 us (7%)
  starting transfers between devices  9.95 us (5%)
    all_gather x1, waiting for transfers between devices, on_device(): gathered = lax.all_gather(keys_values, 'tensor', axis=1, tiled=True)  58 us
    all_to_all x1, waiting for transfers between devices, on_device(): lax.all_to_all(outgoing, 'dp', split_axis=0, concat_axis=0, tiled=True)  49.9 us
    sub x16, matrix products, attend(): powers = jnp.exp(scores - row_max)  20.3 us
    dot_general x16, matrix products, attend(): jnp.einsum('shd,td->hst', query_rows, key_rows, preferred_element_type=jn...  18.6 us
    dot_general x16, matrix products, attend(): jnp.einsum('hst,td->shd', weights, value_rows, preferred_element_type=jnp...  18 us
    all_to_all x1, starting transfers between devices, on_device(): lax.all_to_all(outgoing, 'dp', split_axis=0, concat_axis=0, tiled=True)  9.95 us
    unnamed x10, local copies, waits for them, and re-layouts  8.91 us
  transfers between devices with their start and end apart: 2, of which 2 were waited for; matrix products, arithmetic and copies ran while one was open for 3% of the time, Pallas kernels for 0%

commit v1 on v0

v1 whole, which is shorter than its diff:
```python
import functools
import math

import jax
import jax.numpy as jnp
from jax import lax
from jax.experimental import pallas as pl
from jax.experimental.pallas import tpu as pltpu
from jax.sharding import PartitionSpec as P

MESH = pl.DeviceIdType.MESH
HSIZE = 128
PROMPTS_DEV = 16
SEQ = 256
NZ, NX, NY = 8, 4, 8
NDP = NZ * NX
PIECE = 16
CHUNK = 32
LAST = 2 * NY
RATE = math.log2(math.e) / math.sqrt(HSIZE)


def attend(query_rows, key_rows, value_rows, first):
    scores = lax.dot_general(
        query_rows, key_rows, (((1,), (1,)), ((), ())), preferred_element_type=jnp.float32
    )
    rows = lax.broadcasted_iota(jnp.int32, scores.shape, 0) + first
    columns = lax.broadcasted_iota(jnp.int32, scores.shape, 1)
    scores = jnp.where(rows >= columns, scores, -jnp.inf)
    row_max = jnp.max(scores, axis=1, keepdims=True)
    powers = jnp.exp2((scores - row_max) * RATE)
    weights = (powers * (1.0 / jnp.sum(powers, axis=1, keepdims=True))).astype(jnp.bfloat16)
    return jnp.dot(weights, value_rows, preferred_element_type=jnp.float32).astype(jnp.bfloat16)


def kernel(
    q_ref, kv_ref, donors_ref, ablated_ref, out_ref,
    q_buf, kv_buf, own_buf, send_buf, recv_buf, row_tab,
    q_sem, own_sem, first_send, near_send, twin_send, kv_recv, dp_send, dp_recv,
):
    dp = lax.axis_index("dp")
    tensor = lax.axis_index("tensor")
    z, x = dp // NX, dp % NX
    y, core = tensor // 2, tensor % 2
    group = y // 2
    sign = 1 - 2 * (y % 2)
    near = y + sign
    twin = 1 - core

    def in_group(chip, c):
        return (dp, (chip + 2 * NY) % NY * 2 + c)

    def partner(slot, direction):
        to_z = (z + direction * (slot // NX) + NZ) % NZ
        to_x = (x + direction * (slot % NX) + NX) % NX
        return (to_z * NX + to_x, tensor)

    barrier = pltpu.get_barrier_semaphore()
    for target in [in_group(y - sign * i, core) for i in (1, 2, 3)] + [in_group(near, core), in_group(y, twin)]:
        pl.semaphore_signal(barrier, inc=1, device_id=target, device_id_type=MESH)

    def greet(slot, carry):
        pl.semaphore_signal(barrier, inc=1, device_id=partner(slot, -1), device_id_type=MESH)
        return carry

    lax.fori_loop(1, NDP, greet, 0)

    q_copies = [
        pltpu.make_async_copy(q_ref.at[:, :, pl.ds(i * HSIZE, HSIZE)], q_buf.at[i], q_sem.at[i])
        for i in range(2)
    ]
    for copy in q_copies:
        copy.start()
    own_copy = pltpu.make_async_copy(kv_ref.at[group], kv_buf.at[tensor], own_sem)
    own_copy.start()

    head = ablated_ref[tensor] % 2

    def find_row(slot, carry):
        dest = ((z + slot // NX) % NZ) * NX + (x + slot % NX) % NX
        row = 0
        for p in range(PROMPTS_DEV):
            donor = donors_ref[tensor, dest * PROMPTS_DEV + p]
            row = row + jnp.where(donor // PROMPTS_DEV == dp, donor % PROMPTS_DEV, 0)
        row_tab[slot] = row
        return carry

    lax.fori_loop(0, NDP, find_row, 0)

    pl.semaphore_wait(barrier, NDP - 1 + 5)

    first_copies = []
    for i, step in enumerate((-1, 2, -3)):
        chip = (y + sign * step + 2 * NY) % NY
        first_copies.append(
            pltpu.make_async_remote_copy(
                src_ref=kv_ref.at[chip // 2],
                dst_ref=kv_buf.at[tensor],
                send_sem=first_send.at[i],
                recv_sem=kv_recv.at[tensor],
                device_id=in_group(chip, core),
                device_id_type=MESH,
            )
        )

    def forward(piece, sem, target):
        return pltpu.make_async_remote_copy(
            src_ref=kv_buf.at[piece],
            dst_ref=kv_buf.at[piece],
            send_sem=sem,
            recv_sem=kv_recv.at[piece],
            device_id=target,
            device_id_type=MESH,
        )

    def near_copy(ch):
        return forward(2 * ch + core, near_send.at[ch], in_group(near, core))

    def twin_copy(ch):
        return forward(2 * ch + core, twin_send.at[ch], in_group(y, twin))

    def place(ch):
        return (sign * (y - ch) + 2 * NY) % NY

    for copy in first_copies:
        copy.start()
    own_copy.wait()

    def head_rows(p, start, size, which):
        return q_buf[which, p, start : start + size]

    def keys_of(p, part, length):
        return kv_buf[0 : length // PIECE, part, p].reshape(length, HSIZE)

    for ch in range(NY):
        start, length = ch * CHUNK, (ch + 1) * CHUNK

        @pl.when(place(ch) != 0)
        def _():
            forward(2 * ch + core, near_send.at[ch], in_group(near, core)).wait_recv()

        @pl.when(place(ch) < 4)
        def _():
            near_copy(ch).start()

        twin_copy(ch).start()
        forward(2 * ch + twin, twin_send.at[ch], in_group(y, twin)).wait_recv()
        if ch == 0:
            for copy in q_copies:
                copy.wait()

        def one_prompt(p, carry):
            own_buf[p, start:length] = attend(
                head_rows(p, start, CHUNK, head), keys_of(p, 0, length), keys_of(p, 1, length), start
            )
            return carry

        lax.fori_loop(0, PROMPTS_DEV, one_prompt, 0, unroll=4)

        recv_buf[0, start:length] = own_buf[row_tab[0], start:length]

        def send(slot, carry):
            send_buf[slot, start:length] = own_buf[row_tab[slot], start:length]
            pltpu.make_async_remote_copy(
                src_ref=send_buf.at[slot, pl.ds(start, CHUNK)],
                dst_ref=recv_buf.at[slot, pl.ds(start, CHUNK)],
                send_sem=dp_send,
                recv_sem=dp_recv,
                device_id=partner(slot, 1),
                device_id_type=MESH,
            ).start()
            return carry

        lax.fori_loop(1, NDP, send, 0)

    for copy in first_copies:
        copy.wait_send()
    for ch in range(NY):
        twin_copy(ch).wait_send()

        @pl.when(place(ch) < 4)
        def _():
            near_copy(ch).wait_send()

    half = SEQ // 2

    def other_head(p, carry):
        for start in (0, half):
            length = start + half
            rows = attend(
                head_rows(p, start, half, 1 - head), keys_of(p, 0, length), keys_of(p, 1, length), start
            )
            out_ref[p, start:length, 0:HSIZE] = rows
            out_ref[p, start:length, HSIZE:] = rows
        return carry

    lax.fori_loop(0, PROMPTS_DEV, other_head, 0)

    everything = pltpu.make_async_remote_copy(
        src_ref=send_buf.at[pl.ds(1, NDP - 1)],
        dst_ref=recv_buf.at[pl.ds(1, NDP - 1)],
        send_sem=dp_send,
        recv_sem=dp_recv,
        device_id=partner(1, 1),
        device_id_type=MESH,
    )
    everything.wait()

    def patch(p, carry):
        source = donors_ref[tensor, dp * PROMPTS_DEV + p] // PROMPTS_DEV
        slot = ((z - source // NX + NZ) % NZ) * NX + (x - source % NX + NX) % NX
        block = recv_buf[slot]
        lower = jnp.full(block.shape, head, jnp.int32) == 0
        out_ref[p, :, 0:HSIZE] = jnp.where(lower, block, out_ref[p, :, 0:HSIZE])
        out_ref[p, :, HSIZE:] = jnp.where(lower, out_ref[p, :, HSIZE:], block)
        return carry

    lax.fori_loop(0, PROMPTS_DEV, patch, 0)


def on_device(queries, keys_values, donors, ablated):
    prompts, length, width = queries.shape
    pieces = keys_values.reshape(prompts, PIECE, 2, 4, HSIZE).transpose(3, 2, 0, 1, 4)
    anywhere = pl.BlockSpec(memory_space=pl.ANY)
    scalars = pl.BlockSpec(memory_space=pltpu.SMEM)
    dma = pltpu.SemaphoreType.DMA
    return pl.pallas_call(
        kernel,
        out_shape=jax.ShapeDtypeStruct(queries.shape, jnp.bfloat16),
        in_specs=[anywhere, anywhere, scalars, scalars],
        out_specs=pl.BlockSpec(memory_space=pltpu.VMEM),
        scratch_shapes=[
            pltpu.VMEM((2, prompts, length, HSIZE), jnp.bfloat16),
            pltpu.VMEM((LAST, 2, prompts, PIECE, HSIZE), jnp.bfloat16),
            pltpu.VMEM((prompts, length, HSIZE), jnp.bfloat16),
            pltpu.VMEM((NDP, length, HSIZE), jnp.bfloat16),
            pltpu.VMEM((NDP, length, HSIZE), jnp.bfloat16),
            pltpu.SMEM((NDP,), jnp.int32),
            dma((2,)), dma, dma((3,)), dma((NY,)), dma((NY,)), dma((LAST,)), dma, dma,
        ],
        compiler_params=pltpu.CompilerParams(
            collective_id=0, has_side_effects=True, vmem_limit_bytes=40 * 2**20
        ),
    )(queries, pieces, donors.T, ablated)


def solution(mesh):
    return jax.shard_map(
        on_device,
        mesh=mesh,
        in_specs=(P("dp", None, "tensor"), P("dp", "tensor", None, None), P(), P()),
        out_specs=P("dp", None, "tensor"),
        check_vma=False,
    )
```

time: 214 us -> 116 us (0.54)
  the two profiles are of different devices: /device:TPU:5 before, /device:TPU:33 now
where the time goes in v1:
time: 116 us
  Pallas kernels  112 us (97%)
  local copies, waits for them, and re-layouts  3.82 us (3%)
    pallas_call x1, Pallas kernels, on_device(): pl.pallas_call(kernel, out_shape=jax.ShapeDtypeStruct(queries.shape, jnp....  112 us

profile of v1, /device:TPU:33, one launch (start us, length us, event | category | flops | bytes accessed | tf_op | source)
XLA Modules:
  0.0 116.1 jit_solution(5581408300934102024)
XLA Ops:
  0.0 0.0 copy-start.2
  0.0 0.0 copy-start
  0.0 1.5 %reshape.4 = bf16[16,16,2,4,128]{4,3,2,1,0:T(4,128)(2,1)S(1)} reshape(bf16[16,16,2,512]{3,2,1,0:T(2,128)(2,1)} %param.5) | data formatting | bytes 1048576 | tf_op jit(solution)/shard_map/reshape | solution.py:223
  1.5 0.1 copy.10
  1.6 0.0 copy-done.2
  1.6 0.1 copy-done
  1.8 0.0 copy-start.1
  1.8 0.8 copy-done.1
  2.5 112.2 %shard_map.46 = bf16[16,256,256]{2,1,0:T(8,128)(2,1)S(1)} custom-call(bf16[16,256,256]{2,1,0:T(8,128)(2,1)S(1)} %copy-done, bf16[4,2,16,16,128]{4,3,2,1,0:T(8,128)(2,1)S(1)} %bitcast.4, s32[16,512]{1,0:T(8,128)S(1)} %bitcast.5, s32[16]{0:T(128)S(1)} %copy-done.2), custom_call_target="tpu_custom_call" | custom-call | tf_op jit(solution)/shard_map/pallas_call | solution.py:227
  114.8 1.3 %copy.12 = bf16[16,256,256]{2,1,0:T(8,128)(2,1)} copy(bf16[16,256,256]{2,1,0:T(8,128)(2,1)S(1)} %shard_map.46) | data formatting | bytes 4194304
Async XLA Ops:
  0.0 1.6 %copy-start.2 = (s32[16]{0:T(128)S(1)}, s32[16]{0:T(128)}, u32[]{:S(2)}) copy-start(s32[16]{0:T(128)} %ablated_ref.1) | copy-start | bytes 196
  0.0 1.8 %copy-start = (bf16[16,256,256]{2,1,0:T(8,128)(2,1)S(1)}, bf16[16,256,256]{2,1,0:T(8,128)(2,1)}, u32[]{:S(2)}) copy-start(bf16[16,256,256]{2,1,0:T(8,128)(2,1)} %q_ref.1) | copy-start | bytes 6291460
  1.8 0.8 copy-start.1

commit v2 on v1

v2 whole, which is shorter than its diff:
```python
import functools
import math

import jax
import jax.numpy as jnp
from jax import lax
from jax.experimental import pallas as pl
from jax.experimental.pallas import tpu as pltpu
from jax.sharding import PartitionSpec as P

MESH = pl.DeviceIdType.MESH
HSIZE = 128
PROMPTS_DEV = 16
SEQ = 256
NZ, NX, NY = 8, 4, 8
NDP = NZ * NX
PIECE = 16
CHIP = 2 * PIECE
CHUNKS = ((0, 64, 4), (64, 128, 4), (128, 256, 2))
WAVES = ((0, 4), (4, 8))
LAST = 2 * NY
RATE = math.log2(math.e) / math.sqrt(HSIZE)


def attend(query_rows, key_rows, value_rows, first):
    scores = lax.dot_general(
        query_rows, key_rows, (((1,), (1,)), ((), ())), preferred_element_type=jnp.float32
    )
    rows = lax.broadcasted_iota(jnp.int32, scores.shape, 0) + first
    columns = lax.broadcasted_iota(jnp.int32, scores.shape, 1)
    scores = jnp.where(rows >= columns, scores, -jnp.inf)
    row_max = jnp.max(scores, axis=1, keepdims=True)
    powers = jnp.exp2((scores - row_max) * RATE)
    weights = (powers * (1.0 / jnp.sum(powers, axis=1, keepdims=True))).astype(jnp.bfloat16)
    return jnp.dot(weights, value_rows, preferred_element_type=jnp.float32).astype(jnp.bfloat16)


def kernel(
    q_ref, kv_ref, donors_hbm, ablated_ref, out_ref,
    q_buf, kv_buf, own_buf, send_buf, recv_bufs, donors_ref, row_tab, slot_tab,
    q_sem, own_sem, table_sem, first_send, near_send, twin_send, kv_recv, dp_send, dp_recv,
):
    dp = lax.axis_index("dp")
    tensor = lax.axis_index("tensor")
    z, x = lax.div(dp, NX), lax.rem(dp, NX)
    y, core = lax.div(tensor, 2), lax.rem(tensor, 2)
    group = lax.div(y, 2)
    sign = 1 - 2 * lax.rem(y, 2)
    near = y + sign
    twin = 1 - core

    def in_group(chip, c):
        return (dp, lax.rem(chip + 2 * NY, NY) * 2 + c)

    def shifted(slot, direction):
        to_z = lax.rem(z + direction * lax.div(slot, NX) + NZ, NZ)
        to_x = lax.rem(x + direction * lax.rem(slot, NX) + NX, NX)
        return to_z * NX + to_x

    barrier = pltpu.get_barrier_semaphore()
    for target in [in_group(y - sign * i, core) for i in (1, 2, 3)] + [in_group(near, core), in_group(y, twin)]:
        pl.semaphore_signal(barrier, inc=1, device_id=target, device_id_type=MESH)

    def greet(slot, carry):
        pl.semaphore_signal(barrier, inc=1, device_id=(shifted(slot, -1), tensor), device_id_type=MESH)
        return carry

    lax.fori_loop(1, NDP, greet, 0)

    q_copies = [
        pltpu.make_async_copy(q_ref.at[:, :, pl.ds(i * HSIZE, HSIZE)], q_buf.at[i], q_sem.at[i])
        for i in range(2)
    ]
    for copy in q_copies:
        copy.start()
    own_copy = pltpu.make_async_copy(kv_ref.at[group], kv_buf.at[tensor], own_sem)
    own_copy.start()
    table_copy = pltpu.make_async_copy(donors_hbm, donors_ref, table_sem)
    table_copy.start()

    pl.semaphore_wait(barrier, NDP - 1 + 5)

    def first_copies():
        copies = []
        for i, step in enumerate((-1, 2, -3)):
            chip = lax.rem(y + sign * step + 2 * NY, NY)
            copies.append(
                pltpu.make_async_remote_copy(
                    src_ref=kv_ref.at[lax.div(chip, 2)],
                    dst_ref=kv_buf.at[tensor],
                    send_sem=first_send.at[i],
                    recv_sem=kv_recv.at[tensor],
                    device_id=in_group(chip, core),
                    device_id_type=MESH,
                )
            )
        return copies

    def forward(source, piece, sem, target):
        return pltpu.make_async_remote_copy(
            src_ref=source,
            dst_ref=kv_buf.at[piece],
            send_sem=sem,
            recv_sem=kv_recv.at[piece],
            device_id=target,
            device_id_type=MESH,
        )

    def handled(i):
        return lax.rem(y - sign * i + 2 * NY, NY)

    def passed(i):
        return lax.rem(near + sign * i + 2 * NY, NY)

    def near_copy(i, source):
        return forward(source, 2 * handled(i) + core, near_send.at[i], in_group(near, core))

    def twin_copy(ch, source):
        return forward(source, 2 * ch + core, twin_send.at[ch], in_group(y, twin))

    def take(i):
        ch = handled(i)
        piece = kv_buf.at[2 * ch + core]
        near_copy(i, piece).wait_recv()
        near_copy(i, piece).start()
        twin_copy(ch, piece).start()

    def take_passed(i):
        ch = passed(i)
        piece = kv_buf.at[2 * ch + core]
        twin_copy(ch, piece).wait_recv()
        twin_copy(ch, piece).start()

    def when_in(chips, ch, action, *values):
        first, last = chips
        pl.when(jnp.logical_and(ch >= first, ch < last))(lambda: action(*values))

    def start_own():
        for copy in [near_copy(0, kv_ref.at[group]), twin_copy(y, kv_ref.at[group])] + first_copies():
            copy.start()

    def pass_on(chips):
        when_in(chips, passed(0), take_passed, 0)
        for i in (1, 2, 3):
            when_in(chips, handled(i), take, i)
            when_in(chips, passed(i), take_passed, i)

    def arrive(chips):
        for ch in range(*chips):
            piece = 2 * ch + twin
            forward(kv_buf.at[piece], piece, twin_send.at[ch], in_group(y, twin)).wait_recv()

    start_own()
    own_copy.wait()

    table_copy.wait()
    head = lax.rem(ablated_ref[tensor], 2)

    def find_row(slot, carry):
        dest = shifted(slot, 1)
        row = 0
        for p in range(PROMPTS_DEV):
            donor = donors_ref[tensor, dest * PROMPTS_DEV + p]
            row = row + jnp.where(lax.div(donor, PROMPTS_DEV) == dp, lax.rem(donor, PROMPTS_DEV), 0)
        row_tab[slot] = row
        return carry

    lax.fori_loop(0, NDP, find_row, 0)

    def find_slot(p, carry):
        source = lax.div(donors_ref[tensor, dp * PROMPTS_DEV + p], PROMPTS_DEV)
        slot_z = lax.rem(z - lax.div(source, NX) + NZ, NZ)
        slot_tab[p] = slot_z * NX + lax.rem(x - lax.rem(source, NX) + NX, NX)
        return carry

    lax.fori_loop(0, PROMPTS_DEV, find_slot, 0)

    def keys_of(p, part, length):
        return kv_buf[0 : length // PIECE, part, p].reshape(length, HSIZE)

    def ablated_chunk(start, length, batch):
        def prompts(i, carry):
            results = []
            for j in range(batch):
                p = i * batch + j
                results.append(
                    attend(q_buf[head, p, start:length], keys_of(p, 0, length), keys_of(p, 1, length), start)
                )
            for j in range(batch):
                own_buf[i * batch + j, start:length] = results[j]
            return carry

        lax.fori_loop(0, PROMPTS_DEV // batch, prompts, 0)

    def send_chunk(c, start, length):
        size = length - start
        recv_bufs[c][0] = own_buf[row_tab[0], start:length]

        def send(slot, carry):
            block = pl.ds(NDP * start + slot * size, size)
            send_buf[block] = own_buf[row_tab[slot], start:length]
            pltpu.make_async_remote_copy(
                src_ref=send_buf.at[block],
                dst_ref=recv_bufs[c].at[slot],
                send_sem=dp_send.at[c],
                recv_sem=dp_recv.at[c],
                device_id=(shifted(slot, 1), tensor),
                device_id_type=MESH,
            ).start()
            return carry

        lax.fori_loop(1, NDP, send, 0)

    for c, (start, length, batch) in enumerate(CHUNKS):
        wave = [w for w in range(len(WAVES)) if WAVES[w][0] * CHIP == start]
        for w in wave:
            pass_on(WAVES[w])
            arrive(WAVES[w])
        if c == 0:
            for copy in q_copies:
                copy.wait()
        ablated_chunk(start, length, batch)
        send_chunk(c, start, length)

    half = SEQ // 2

    def other_head(p, carry):
        results = []
        for start in (0, half):
            length = start + half
            results.append(
                attend(q_buf[1 - head, p, start:length], keys_of(p, 0, length), keys_of(p, 1, length), start)
            )
        for start, rows in zip((0, half), results):
            out_ref[p, start : start + half, 0:HSIZE] = rows
            out_ref[p, start : start + half, HSIZE:] = rows
        return carry

    lax.fori_loop(0, PROMPTS_DEV, other_head, 0)

    for copy in first_copies():
        copy.wait_send()
    for ch in range(NY):
        twin_copy(ch, kv_buf.at[2 * ch + core]).wait_send()
    for i in range(4):
        near_copy(i, kv_buf.at[2 * handled(i) + core]).wait_send()

    for c, (start, length, batch) in enumerate(CHUNKS):
        size = length - start
        received = recv_bufs[c].at[pl.ds(1, NDP - 1)]
        pltpu.make_async_remote_copy(
            src_ref=received,
            dst_ref=received,
            send_sem=dp_send.at[c],
            recv_sem=dp_recv.at[c],
            device_id=(shifted(1, 1), tensor),
            device_id_type=MESH,
        ).wait()
        lower = jnp.full((size, HSIZE), head, jnp.int32) == 0

        def patch(p, carry):
            block = recv_bufs[c][slot_tab[p]]
            other = out_ref[p, start:length, 0:HSIZE]
            out_ref[p, start:length, 0:HSIZE] = jnp.where(lower, block, other)
            out_ref[p, start:length, HSIZE:] = jnp.where(lower, other, block)
            return carry

        lax.fori_loop(0, PROMPTS_DEV, patch, 0, unroll=2)


def on_device(queries, keys_values, donors, ablated):
    prompts, length, width = queries.shape
    pieces = keys_values.reshape(prompts, PIECE, 2, 4, HSIZE).transpose(3, 2, 0, 1, 4)
    anywhere = pl.BlockSpec(memory_space=pl.ANY)
    scalars = pl.BlockSpec(memory_space=pltpu.SMEM)
    dma = pltpu.SemaphoreType.DMA
    return pl.pallas_call(
        kernel,
        out_shape=jax.ShapeDtypeStruct(queries.shape, jnp.bfloat16),
        in_specs=[anywhere, pl.BlockSpec(memory_space=pltpu.VMEM), anywhere, scalars],
        out_specs=pl.BlockSpec(memory_space=pltpu.VMEM),
        scratch_shapes=[
            pltpu.VMEM((2, prompts, length, HSIZE), jnp.bfloat16),
            pltpu.VMEM((LAST, 2, prompts, PIECE, HSIZE), jnp.bfloat16),
            pltpu.VMEM((prompts, length, HSIZE), jnp.bfloat16),
            pltpu.VMEM((NDP * length, HSIZE), jnp.bfloat16),
            [pltpu.VMEM((NDP, last - start, HSIZE), jnp.bfloat16) for start, last, _ in CHUNKS],
            pltpu.SMEM(donors.shape[::-1], jnp.int32),
            pltpu.SMEM((NDP,), jnp.int32),
            pltpu.SMEM((PROMPTS_DEV,), jnp.int32),
            dma((2,)), dma, dma, dma((3,)), dma((4,)), dma((NY,)), dma((LAST,)), dma((len(CHUNKS),)), dma((len(CHUNKS),)),
        ],
        compiler_params=pltpu.CompilerParams(
            collective_id=0, has_side_effects=True, vmem_limit_bytes=40 * 2**20
        ),
    )(queries, pieces, donors.T, ablated)


def solution(mesh):
    return jax.shard_map(
        on_device,
        mesh=mesh,
        in_specs=(P("dp", None, "tensor"), P("dp", "tensor", None, None), P(), P()),
        out_specs=P("dp", None, "tensor"),
        check_vma=False,
    )
```

time: 116 us -> 92.9 us (0.80)
  the two profiles are of different devices: /device:TPU:33 before, /device:TPU:34 now
where the time goes in v2:
time: 92.9 us; the launch traced here: 92.7 us
  Pallas kernels  88.9 us (96%)
  local copies, waits for them, and re-layouts  3.82 us (4%)
    pallas_call x1, Pallas kernels, on_device(): pl.pallas_call(kernel, out_shape=jax.ShapeDtypeStruct(queries.shape, jnp....  88.9 us
    unnamed x7, local copies, waits for them, and re-layouts  2.23 us

profile of v2, /device:TPU:34, one launch (start us, length us, event | category | flops | bytes accessed | tf_op | source)
XLA Modules:
  0.0 92.7 jit_solution(5346877912010292137)
XLA Ops:
  0.0 0.0 copy-start.2
  0.0 0.0 copy-start
  0.0 1.5 %reshape.4 = bf16[16,16,2,4,128]{4,3,2,1,0:T(4,128)(2,1)S(1)} reshape(bf16[16,16,2,512]{3,2,1,0:T(2,128)(2,1)} %param.5) | data formatting | bytes 1048576 | tf_op jit(solution)/shard_map/reshape | solution.py:273
  1.5 0.1 copy.10
  1.6 0.0 copy-done.2
  1.6 0.1 copy-done
  1.8 0.0 copy-start.1
  1.8 0.8 copy-done.1
  2.5 88.9 %shard_map.46 = bf16[16,256,256]{2,1,0:T(8,128)(2,1)S(1)} custom-call(bf16[16,256,256]{2,1,0:T(8,128)(2,1)S(1)} %copy-done, bf16[4,2,16,16,128]{4,3,2,1,0:T(8,128)(2,1)S(1)} %bitcast.4, s32[16,512]{1,0:T(8,128)S(1)} %bitcast.5, s32[16]{0:T(128)S(1)} %copy-done.2), custom_call_target="tpu_custom_call" | custom-call | tf_op jit(solution)/shard_map/pallas_call | solution.py:277
  91.4 1.3 %copy.12 = bf16[16,256,256]{2,1,0:T(8,128)(2,1)} copy(bf16[16,256,256]{2,1,0:T(8,128)(2,1)S(1)} %shard_map.46) | data formatting | bytes 4194304
Async XLA Ops:
  0.0 1.6 %copy-start.2 = (s32[16]{0:T(128)S(1)}, s32[16]{0:T(128)}, u32[]{:S(2)}) copy-start(s32[16]{0:T(128)} %ablated_ref.1) | copy-start | bytes 196
  0.0 1.8 %copy-start = (bf16[16,256,256]{2,1,0:T(8,128)(2,1)S(1)}, bf16[16,256,256]{2,1,0:T(8,128)(2,1)}, u32[]{:S(2)}) copy-start(bf16[16,256,256]{2,1,0:T(8,128)(2,1)} %q_ref.1) | copy-start | bytes 6291460
  1.8 0.8 copy-start.1

commit v3 on v2

--- a/solution.py
+++ b/solution.py
@@ -16,7 +16,7 @@
 NDP = NZ * NX
 PIECE = 16
 CHIP = 2 * PIECE
-CHUNKS = ((0, 64, 4), (64, 128, 4), (128, 256, 2))
+CHUNKS = ((0, 64, 8), (64, 128, 4), (128, 256, 4))
 WAVES = ((0, 4), (4, 8))
 LAST = 2 * NY
 RATE = math.log2(math.e) / math.sqrt(HSIZE)
@@ -80,31 +80,23 @@
 
     pl.semaphore_wait(barrier, NDP - 1 + 5)
 
-    def first_copies():
+    def forward(source, piece, part, sem, target):
+        return pltpu.make_async_remote_copy(
+            src_ref=source.at[part],
+            dst_ref=kv_buf.at[piece, part],
+            send_sem=sem,
+            recv_sem=kv_recv.at[piece, part],
+            device_id=target,
+            device_id_type=MESH,
+        )
+
+    def first_copies(part):
         copies = []
         for i, step in enumerate((-1, 2, -3)):
             chip = lax.rem(y + sign * step + 2 * NY, NY)
-            copies.append(
-                pltpu.make_async_remote_copy(
-                    src_ref=kv_ref.at[lax.div(chip, 2)],
-                    dst_ref=kv_buf.at[tensor],
-                    send_sem=first_send.at[i],
-                    recv_sem=kv_recv.at[tensor],
-                    device_id=in_group(chip, core),
-                    device_id_type=MESH,
-                )
-            )
+            source = kv_ref.at[lax.div(chip, 2)]
+            copies.append(forward(source, tensor, part, first_send.at[i, part], in_group(chip, core)))
         return copies
-
-    def forward(source, piece, sem, target):
-        return pltpu.make_async_remote_copy(
-            src_ref=source,
-            dst_ref=kv_buf.at[piece],
-            send_sem=sem,
-            recv_sem=kv_recv.at[piece],
-            device_id=target,
-            device_id_type=MESH,
-        )
 
     def handled(i):
         return lax.rem(y - sign * i + 2 * NY, NY)
@@ -112,43 +104,50 @@
     def passed(i):
         return lax.rem(near + sign * i + 2 * NY, NY)
 
-    def near_copy(i, source):
-        return forward(source, 2 * handled(i) + core, near_send.at[i], in_group(near, core))
-
-    def twin_copy(ch, source):
-        return forward(source, 2 * ch + core, twin_send.at[ch], in_group(y, twin))
-
-    def take(i):
+    def near_copy(i, source, part):
+        return forward(source, 2 * handled(i) + core, part, near_send.at[i, part], in_group(near, core))
+
+    def twin_copy(ch, source, part):
+        return forward(source, 2 * ch + core, part, twin_send.at[ch, part], in_group(y, twin))
+
+    def take(i, part):
         ch = handled(i)
         piece = kv_buf.at[2 * ch + core]
-        near_copy(i, piece).wait_recv()
-        near_copy(i, piece).start()
-        twin_copy(ch, piece).start()
-
-    def take_passed(i):
+        near_copy(i, piece, part).wait_recv()
+        near_copy(i, piece, part).start()
+        twin_copy(ch, piece, part).start()
+
+    def take_passed(i, part):
         ch = passed(i)
         piece = kv_buf.at[2 * ch + core]
-        twin_copy(ch, piece).wait_recv()
-        twin_copy(ch, piece).start()
+        twin_copy(ch, piece, part).wait_recv()
+        twin_copy(ch, piece, part).start()
 
     def when_in(chips, ch, action, *values):
         first, last = chips
         pl.when(jnp.logical_and(ch >= first, ch < last))(lambda: action(*values))
 
     def start_own():
-        for copy in [near_copy(0, kv_ref.at[group]), twin_copy(y, kv_ref.at[group])] + first_copies():
-            copy.start()
+        own = kv_ref.at[group]
+        for part in range(2):
+            for copy in [near_copy(0, own, part), twin_copy(y, own, part)] + first_copies(part):
+                copy.start()
 
     def pass_on(chips):
-        when_in(chips, passed(0), take_passed, 0)
-        for i in (1, 2, 3):
-            when_in(chips, handled(i), take, i)
-            when_in(chips, passed(i), take_passed, i)
+        for part in range(2):
+            when_in(chips, passed(0), take_passed, 0, part)
+            for i in (1, 2, 3):
+                when_in(chips, handled(i), take, i, part)
+            for i in (1, 2, 3):
+                when_in(chips, passed(i), take_passed, i, part)
 
     def arrive(chips):
         for ch in range(*chips):
-            piece = 2 * ch + twin
-            forward(kv_buf.at[piece], piece, twin_send.at[ch], in_group(y, twin)).wait_recv()
+            for part in range(2):
+                piece = 2 * ch + twin
+                forward(
+                    kv_buf.at[piece], piece, part, twin_send.at[ch, part], in_group(y, twin)
+                ).wait_recv()
 
     start_own()
     own_copy.wait()
@@ -238,12 +237,13 @@
 
     lax.fori_loop(0, PROMPTS_DEV, other_head, 0)
 
-    for copy in first_copies():
-        copy.wait_send()
-    for ch in range(NY):
-        twin_copy(ch, kv_buf.at[2 * ch + core]).wait_send()
-    for i in range(4):
-        near_copy(i, kv_buf.at[2 * handled(i) + core]).wait_send()
+    for part in range(2):
+        for copy in first_copies(part):
+            copy.wait_send()
+        for ch in range(NY):
+            twin_copy(ch, kv_buf.at[2 * ch + core], part).wait_send()
+        for i in range(4):
+            near_copy(i, kv_buf.at[2 * handled(i) + core], part).wait_send()
 
     for c, (start, length, batch) in enumerate(CHUNKS):
         size = length - start
@@ -288,7 +288,7 @@
             pltpu.SMEM(donors.shape[::-1], jnp.int32),
             pltpu.SMEM((NDP,), jnp.int32),
             pltpu.SMEM((PROMPTS_DEV,), jnp.int32),
-            dma((2,)), dma, dma, dma((3,)), dma((4,)), dma((NY,)), dma((LAST,)), dma((len(CHUNKS),)), dma((len(CHUNKS),)),
+            dma((2,)), dma, dma, dma((3, 2)), dma((4, 2)), dma((NY, 2)), dma((LAST, 2)), dma((len(CHUNKS),)), dma((len(CHUNKS),)),
         ],
         compiler_params=pltpu.CompilerParams(
             collective_id=0, has_side_effects=True, vmem_limit_bytes=40 * 2**20

time: 92.9 us -> 90.7 us (0.976)
  the two profiles are of different devices: /device:TPU:34 before, /device:TPU:41 now
where the time goes in v3:
time: 90.7 us; the launch traced here: 90.5 us
  Pallas kernels  86.6 us (95%)
  local copies, waits for them, and re-layouts  3.82 us (4%)
    pallas_call x1, Pallas kernels, on_device(): pl.pallas_call(kernel, out_shape=jax.ShapeDtypeStruct(queries.shape, jnp....  86.6 us
    unnamed x7, local copies, waits for them, and re-layouts  2.23 us

profile of v3, /device:TPU:41, one launch (start us, length us, event | category | flops | bytes accessed | tf_op | source)
XLA Modules:
  0.0 90.5 jit_solution(17880206600586376774)
XLA Ops:
  0.0 0.0 copy-start.2
  0.0 0.0 copy-start
  0.0 1.5 %reshape.4 = bf16[16,16,2,4,128]{4,3,2,1,0:T(4,128)(2,1)S(1)} reshape(bf16[16,16,2,512]{3,2,1,0:T(2,128)(2,1)} %param.5) | data formatting | bytes 1048576 | tf_op jit(solution)/shard_map/reshape | solution.py:273
  1.5 0.1 copy.10
  1.6 0.0 copy-done.2
  1.6 0.1 copy-done
  1.8 0.0 copy-start.1
  1.8 0.8 copy-done.1
  2.5 86.6 %shard_map.46 = bf16[16,256,256]{2,1,0:T(8,128)(2,1)S(1)} custom-call(bf16[16,256,256]{2,1,0:T(8,128)(2,1)S(1)} %copy-done, bf16[4,2,16,16,128]{4,3,2,1,0:T(8,128)(2,1)S(1)} %bitcast.4, s32[16,512]{1,0:T(8,128)S(1)} %bitcast.5, s32[16]{0:T(128)S(1)} %copy-done.2), custom_call_target="tpu_custom_call" | custom-call | tf_op jit(solution)/shard_map/pallas_call | solution.py:277
  89.1 1.3 %copy.12 = bf16[16,256,256]{2,1,0:T(8,128)(2,1)} copy(bf16[16,256,256]{2,1,0:T(8,128)(2,1)S(1)} %shard_map.46) | data formatting | bytes 4194304
Async XLA Ops:
  0.0 1.6 %copy-start.2 = (s32[16]{0:T(128)S(1)}, s32[16]{0:T(128)}, u32[]{:S(2)}) copy-start(s32[16]{0:T(128)} %ablated_ref.1) | copy-start | bytes 196
  0.0 1.8 %copy-start = (bf16[16,256,256]{2,1,0:T(8,128)(2,1)S(1)}, bf16[16,256,256]{2,1,0:T(8,128)(2,1)}, u32[]{:S(2)}) copy-start(bf16[16,256,256]{2,1,0:T(8,128)(2,1)} %q_ref.1) | copy-start | bytes 6291460
  1.8 0.8 copy-start.1

commit v4 on v3

--- a/solution.py
+++ b/solution.py
@@ -16,7 +16,7 @@
 NDP = NZ * NX
 PIECE = 16
 CHIP = 2 * PIECE
-CHUNKS = ((0, 64, 8), (64, 128, 4), (128, 256, 4))
+CHUNKS = ((0, 64, 8), (64, 128, 8), (128, 256, 4))
 WAVES = ((0, 4), (4, 8))
 LAST = 2 * NY
 RATE = math.log2(math.e) / math.sqrt(HSIZE)
@@ -214,7 +214,7 @@
         wave = [w for w in range(len(WAVES)) if WAVES[w][0] * CHIP == start]
         for w in wave:
             pass_on(WAVES[w])
-            arrive(WAVES[w])
+        arrive((start // CHIP, length // CHIP))
         if c == 0:
             for copy in q_copies:
                 copy.wait()
@@ -291,7 +291,7 @@
             dma((2,)), dma, dma, dma((3, 2)), dma((4, 2)), dma((NY, 2)), dma((LAST, 2)), dma((len(CHUNKS),)), dma((len(CHUNKS),)),
         ],
         compiler_params=pltpu.CompilerParams(
-            collective_id=0, has_side_effects=True, vmem_limit_bytes=40 * 2**20
+            collective_id=0, has_side_effects=True, vmem_limit_bytes=60 * 2**20
         ),
     )(queries, pieces, donors.T, ablated)
 

time: 90.7 us -> 94 us (1.036)
  Pallas kernels: 86.6 us -> 88.5 us
  local copies, waits for them, and re-layouts: 3.82 us -> 5.35 us
    pallas_call x1, Pallas kernels: 86.6 us -> 88.5 us  [on_device(): pl.pallas_call(kernel, out_shape=jax.ShapeDtypeStruct(queries.shape, jnp....]
    unnamed x7 -> x1, local copies, waits for them, and re-layouts: 2.23 us -> 3.1 us
where the time goes in v4:
time: 94 us; the launch traced here: 93.8 us
  Pallas kernels  88.5 us (94%)
  local copies, waits for them, and re-layouts  5.35 us (6%)
    pallas_call x1, Pallas kernels, on_device(): pl.pallas_call(kernel, out_shape=jax.ShapeDtypeStruct(queries.shape, jnp....  88.5 us
    unnamed x1, local copies, waits for them, and re-layouts  3.1 us
    reshape x2, local copies, waits for them, and re-layouts, on_device(): keys_values.reshape(prompts, PIECE, 2, 4, HSIZE).transpose(3, 2, 0, 1, 4)  2.25 us

profile of v4, /device:TPU:41, one launch (start us, length us, event | category | flops | bytes accessed | tf_op | source)
XLA Modules:
  0.0 93.8 jit_solution(3870370371153466993)
XLA Ops:
  0.0 1.4 %reshape.4 = bf16[16,16,2,4,128]{4,3,2,1,0:T(4,128)(2,1)S(1)} reshape(bf16[16,16,2,512]{3,2,1,0:T(2,128)(2,1)} %param.5) | data formatting | bytes 1048576 | tf_op jit(solution)/shard_map/reshape | solution.py:273
  1.4 0.9 copy.10
  2.3 88.5 %shard_map.46 = bf16[16,256,256]{2,1,0:T(8,128)(2,1)} custom-call(bf16[16,256,256]{2,1,0:T(8,128)(2,1)} %q_ref.1, bf16[4,2,16,16,128]{4,3,2,1,0:T(8,128)(2,1)} %bitcast.4, s32[16,512]{1,0:T(8,128)} %bitcast.5, s32[16]{0:T(128)} %ablated_ref.1), custom_call_target="tpu_custom_call" | custom-call | tf_op jit(solution)/shard_map/pallas_call | solution.py:277
  90.7 3.1 %copy.12 = bf16[16,256,256]{2,1,0:T(8,128)(2,1)} copy(bf16[16,256,256]{2,1,0:T(8,128)(2,1)} %shard_map.46) | data formatting | bytes 4194304
